TPU v7x, 32 devices: a whole 2x2x4 slice. The times are simulated.
32 devices in a mesh: section: 4 (over x, core), dp: 8 (over z, y).
Axes of the slice: x: 2, y: 2, z: 4, core: 2. Of those that a mesh axis runs over, the one named last changes fastest.
Arguments:
- layer_inputs: bfloat16 [4, 8, 512, 4096], P('section', 'dp'), may hold values from -6 to 6
- out_grads: bfloat16 [4, 8, 512, 4096], P('section', 'dp'), may hold values from -6 to 6
- projections: bfloat16 [4, 4096, 128], P('section'), may hold values from -0.09375 to 0.09375
- query_grads: bfloat16 [4, 256, 4096], P('section', 'dp'), may hold values from -0.59765625 to 0.59765625
- lengths: int32 [8], P('dp'), may hold values from 1 to 512, as said below
Outputs:
- scores: float32 [8, 256], P('dp', 'section')
Inputs may be any that keep to these rules, and one draw needn't show every extreme that they name: `lengths`: some training example fills all 512 slots.
All inputs are finite; a program needn't handle non-finite values.
Results may differ from a plain program's by a relative error of at most 0.005.
Values may be sent and summed in bfloat16 or wider, within the bound.
A program may use at most 128 MiB of HBM per device.

v0:
```python
import jax
import jax.numpy as jnp
from jax import lax
from jax.sharding import PartitionSpec as P


def project_layer(inputs, grads, proj_table, valid_mask, token_count):
    low_rank = proj_table.shape[1] // 2
    ex_rows, seq_len, model_width = inputs.shape
    input_side = jnp.dot(
        inputs.reshape(ex_rows * seq_len, model_width),
        proj_table[:, :low_rank],
        preferred_element_type=jnp.float32,
    )
    input_side = input_side.astype(jnp.bfloat16).reshape(ex_rows, seq_len, low_rank)
    grad_side = jnp.dot(
        grads.reshape(ex_rows * seq_len, model_width),
        proj_table[:, low_rank:],
        preferred_element_type=jnp.float32,
    )
    grad_side = grad_side.astype(jnp.bfloat16).reshape(ex_rows, seq_len, low_rank)
    masked = grad_side * valid_mask[:, :, None]
    summed = (
        jnp.einsum("esa,esb->eab", masked, input_side, preferred_element_type=jnp.float32)
        / token_count[:, None, None]
    )
    return summed.astype(jnp.bfloat16).reshape(ex_rows, low_rank * low_rank)


def on_device(layer_inputs, out_grads, projections, query_grads, lengths):
    seq_len = layer_inputs.shape[2]
    valid_mask = (
        lax.broadcasted_iota(jnp.int32, (lengths.shape[0], seq_len), 1) < lengths[:, None]
    ).astype(jnp.bfloat16)
    token_count = lengths.astype(jnp.float32)
    example_grads = jnp.stack(
        [project_layer(layer_inputs[0], out_grads[0], projections[0], valid_mask, token_count)]
    )
    score_block = jnp.einsum(
        "ler,lqr->eq",
        lax.all_gather(example_grads, "dp", axis=1, tiled=True),
        query_grads,
        preferred_element_type=jnp.float32,
    )
    partial_value = lax.all_to_all(score_block, "dp", split_axis=0, concat_axis=1, tiled=True)
    return lax.psum_scatter(partial_value, "section", scatter_dimension=1, tiled=True)


def solution(mesh):
    placed = (
        P("section", "dp", None, None),
        P("section", "dp", None, None),
        P("section", None, None),
        P("section", "dp", None),
        P("dp"),
    )
    return jax.shard_map(
        on_device, mesh=mesh, in_specs=placed, out_specs=P("dp", "section"), check_vma=False
    )
```

profile of v0, /device:TPU:0, one launch (start us, length us, event | category | flops | bytes accessed | tf_op | source)
XLA Modules:
  0.0 86.8 jit_solution(7748604327050533801)
XLA Ops:
  6.5 0.0 copy-start
  6.5 0.0 copy-start.1
  6.5 0.0 reduce-scatter.4.cloned.1.call-start
  7.3 4.2 %fusion.13 = bf16[512,64]{0,1:T(8,128)(2,1)S(1)} fusion(bf16[1,1,512,4096]{3,2,1,0:T(8,128)(2,1)} %param.6, bf16[4096,128]{1,0:T(8,128)(2,1)} %bitcast.35, bf16[512]{0:T(512)(128)(2,1)S(1)} %fusion.29), kind=kOutput, calls=%fused_computation.7 | convolution fusion | flops 268500992 | bytes 5309440 | tf_op jit(solution)/shard_map/dot_general | solution.py:16
  11.5 0.0 copy-done.1
  11.5 3.7 %fusion.19 = bf16[64,64]{1,0:T(8,128)(2,1)S(1)} fusion(bf16[512,64]{0,1:T(8,128)(2,1)S(1)} %fusion.13, bf16[1,1,512,4096]{3,2,1,0:T(8,128)(2,1)} %param.5, bf16[4096,128]{1,0:T(8,128)(2,1)S(1)} %bitcast.36, f32[]{:T(128)} %bitcast.4), kind=kOutput, calls=%fused_computation.9 | convolution fusion | flops 272670720 | bytes 5316612 | tf_op jit(solution)/shard_map/esa,esb->eab/dot_general | solution.py:24
  15.3 0.1 stack_reshape.3
  15.3 32.3 %all_gather.3 = bf16[1,8,4096]{2,0,1:T(2,128)(2,1)S(1)} all-gather(bf16[1,1,4096]{2,0,1:T(2,128)(2,1)S(1)} %bitcast.38), channel_id=1, replica_groups=mesh['section'=4,'dp'=8] {'dp'}, dimensions={1}, use_global_device_ids=true | all-gather | bytes 73728 | tf_op jit(solution)/shard_map/all_gather | solution.py:41
  47.7 0.0 copy-done
  47.7 0.2 fusion.25
  47.9 11.8 %all_to_all.17 = f32[8,1,32]{2,1,0:T(1,128)S(1)} all-to-all(f32[8,1,32]{2,1,0:T(1,128)S(1)} %bitcast.40), channel_id=1, replica_groups=mesh['section'=4,'dp'=8] {'dp'}, dimensions={0} | all-to-all | bytes 2048 | tf_op jit(solution)/shard_map/all_to_all | solution.py:45
  59.6 0.5 broadcast.14
  60.2 0.7 reduce.3
  60.8 0.8 all_to_all.15
  61.6 0.0 reduce-scatter.4.cloned.1.call-update
  61.6 17.0 %reduce-scatter.4.cloned.1.call-done = f32[64,1]{1,0:T(8,128)} async-done(((f32[256,1]{1,0:T(8,128)}), f32[64,1]{1,0:T(8,128)}) %reduce-scatter.4.cloned.1.call-update) | async-done | bytes 272
  78.6 1.3 %copy.11 = f32[1,64]{1,0:T(1,128)} copy(f32[1,64]{0,1:T(8,128)} %bitcast.39) | data formatting | bytes 512
  (1 shorter events, 0.0 us)
Async XLA Ops:
  6.5 41.1 %copy-start = (bf16[1,32,4096]{2,1,0:T(8,128)(2,1)S(1)}, bf16[1,32,4096]{2,1,0:T(8,128)(2,1)}, u32[]{:S(2)}) copy-start(bf16[1,32,4096]{2,1,0:T(8,128)(2,1)} %param.8) | copy-start | bytes 786436
  6.5 5.0 %copy-start.1 = (bf16[1,4096,128]{2,1,0:T(8,128)(2,1)S(1)}, bf16[1,4096,128]{2,1,0:T(8,128)(2,1)}, u32[]{:S(2)}) copy-start(bf16[1,4096,128]{2,1,0:T(8,128)(2,1)} %param.7) | copy-start | bytes 3145732
  6.5 72.1 %reduce-scatter.4.cloned.1.call-start = ((), (), s32[]{:S(2)}) async-start(), calls=%async_computation.2 | async-start | bytes 163840
Sparse Core Ops, SparseCore 0:
  61.7 16.8 reduce-scatter.3
where the time goes:
time: 87.1 us; the launch traced here: 86.8 us
  blocking collectives  44.1 us (51%)
  waiting for transfers between devices  17 us (20%)
  between operations  14.2 us (16%)
  matrix products  8.15 us (9%)
  local copies, waits for them, and re-layouts  2.72 us (3%)
    all_gather x1, blocking collectives, on_device(): lax.all_gather(example_grads, 'dp', axis=1, tiled=True)  32.3 us
    unnamed x2, waiting for transfers between devices  17 us
    all_to_all x1, blocking collectives, on_device(): lax.all_to_all(score_block, 'dp', split_axis=0, concat_axis=1, tiled=True)  11.8 us
    dot_general x1, matrix products, project_layer(): jnp.dot(grads.reshape(ex_rows * seq_len, model_width), proj_table[:, low_...  4.21 us
    dot_general x1, matrix products, project_layer(): jnp.einsum('esa,esb->eab', masked, input_side, preferred_element_type=jnp...  3.72 us
  transfers between devices with their start and end apart: 1, of which 1 were waited for; matrix products, arithmetic and copies ran while one was open for 0% of the time, Pallas kernels for 0%

commit v1 on v0

v1 whole, which is shorter than its diff:
```python
import functools

import jax
import jax.numpy as jnp
from jax import lax
from jax.experimental import pallas as pl
from jax.experimental.pallas import tpu as pltpu
from jax.sharding import PartitionSpec as P

MESH = pl.DeviceIdType.MESH
CHUNKS = 4


def kernel(
    sections, members, width,
    inputs_ref, grads_ref, proj_ref, query_ref, length_ref, out_ref,
    rows, proj, query, length, product, packed, spread, scores, parts,
    row_sem, proj_sem, query_sem, length_sem,
    grad_send, grad_recv, score_send, score_recv,
):
    sec, dp = lax.axis_index("section"), lax.axis_index("dp")
    seq_len = inputs_ref.shape[2]
    step = seq_len // CHUNKS
    rank = proj_ref.shape[2] // 2
    block = query_ref.shape[1]
    group = members // sections
    per = width // block
    home = dp // group
    keeps = home == sec
    my_slot = (dp % group) // per * (sections * per) + sec * per + dp % per

    length_copy = pltpu.make_async_copy(length_ref, length, length_sem)
    length_copy.start()
    proj_copy = pltpu.make_async_copy(proj_ref.at[0], proj, proj_sem)
    proj_copy.start()
    row_copies = []
    for c in range(CHUNKS):
        span = pl.ds(c * step, step)
        pair = (
            pltpu.make_async_copy(inputs_ref.at[0, 0, span], rows.at[c, pl.ds(0, step)], row_sem.at[c, 0]),
            pltpu.make_async_copy(grads_ref.at[0, 0, span], rows.at[c, pl.ds(step, step)], row_sem.at[c, 1]),
        )
        for copy in pair:
            copy.start()
        row_copies.append(pair)
    query_copies = []
    for k in range(per):
        copy = pltpu.make_async_copy(query_ref.at[0], query.at[pl.ds(k * block, block)], query_sem.at[k])
        copy.start()
        query_copies.append(copy)

    barrier = pltpu.get_barrier_semaphore()

    @pl.loop(1, members)
    def _(k):
        pl.semaphore_signal(
            barrier, inc=1, device_id=(sec, lax.rem(dp + k, members)), device_id_type=MESH
        )

    @pl.loop(0, sections)
    def _(s):
        @pl.loop(0, group)
        def _(g):
            sender = sec * group + g

            @pl.when(jnp.logical_not(jnp.logical_and(s == sec, sender == dp)))
            def _():
                pl.semaphore_signal(barrier, inc=1, device_id=(s, sender), device_id_type=MESH)

    length_copy.wait()
    proj_copy.wait()
    tokens = length[0]
    total = jnp.zeros((2 * rank, 2 * rank), jnp.float32)
    for c in range(CHUNKS):
        for copy in row_copies[c]:
            copy.wait()
        sides = jnp.dot(rows[c], proj[...], preferred_element_type=jnp.float32).astype(jnp.bfloat16)
        slot = lax.broadcasted_iota(jnp.int32, (step, 2 * rank), 0) + c * step
        masked = jnp.where(slot < tokens, sides[step:].astype(jnp.float32), 0.0).astype(jnp.bfloat16)
        total += lax.dot_general(
            masked, sides[:step], (((0,), (0,)), ((), ())), preferred_element_type=jnp.float32
        )
    product[...] = total[rank:]
    half = rank // 2
    even = product[pl.ds(0, half, stride=2), :]
    odd = product[pl.ds(1, half, stride=2), :]
    lane = lax.broadcasted_iota(jnp.int32, (half, 2 * rank), 1)
    folded = jnp.where(lane < rank, even, pltpu.roll(odd, rank, 1))
    packed[dp] = (folded / tokens.astype(jnp.float32)).astype(jnp.bfloat16)

    pl.semaphore_wait(barrier, members - 1 + sections * group - jnp.where(keeps, 1, 0))

    def grad_copy(k):
        return pltpu.make_async_remote_copy(
            src_ref=packed.at[dp], dst_ref=packed.at[dp],
            send_sem=grad_send.at[k], recv_sem=grad_recv.at[k],
            device_id=(sec, lax.rem(dp + k, members)), device_id_type=MESH,
        )

    @pl.loop(1, members)
    def _(k):
        grad_copy(k).start()

    for copy in query_copies:
        copy.wait()

    @pl.loop(1, members)
    def _(k):
        grad_copy(k).wait_recv()

    spread[...] = packed[...].reshape(members * half, 2 * rank).astype(jnp.float32)
    left = jnp.concatenate(
        [spread[pl.ds(i, members, stride=half), :].astype(jnp.bfloat16) for i in range(half)], axis=1
    )
    found = lax.dot_general(
        left, query[...], (((1,), (1,)), ((), ())), preferred_element_type=jnp.float32
    )
    place = lax.broadcasted_iota(jnp.int32, found.shape, 1) // block
    found = jnp.where(place == dp % per, found, 0.0)
    scores[...] = found.reshape(members, 1, width)

    def score_copy(e):
        return pltpu.make_async_remote_copy(
            src_ref=scores.at[e], dst_ref=parts.at[my_slot],
            send_sem=score_send.at[e], recv_sem=score_recv.at[my_slot],
            device_id=(home, e), device_id_type=MESH,
        )

    @pl.loop(0, members)
    def _(k):
        e = lax.rem(dp + k, members)

        @pl.when(jnp.logical_or(jnp.logical_not(keeps), k > 0))
        def _():
            score_copy(e).start()

    @pl.when(keeps)
    def _():
        parts[my_slot] = scores[dp]

    @pl.loop(0, sections * group)
    def _(slot):
        @pl.when(jnp.logical_or(jnp.logical_not(keeps), slot != my_slot))
        def _():
            pltpu.make_async_remote_copy(
                src_ref=scores.at[0], dst_ref=parts.at[slot],
                send_sem=score_send.at[0], recv_sem=score_recv.at[slot],
                device_id=(home, dp), device_id_type=MESH,
            ).wait_recv()

    count = sections * per
    for b in range(group // per):
        piece = parts[b * count]
        for k in range(1, count):
            piece = piece + parts[b * count + k]
        out_ref[:, pl.ds(b * width, width)] = piece

    @pl.loop(1, members)
    def _(k):
        grad_copy(k).wait_send()

    @pl.loop(0, members)
    def _(k):
        @pl.when(jnp.logical_or(jnp.logical_not(keeps), k > 0))
        def _():
            score_copy(lax.rem(dp + k, members)).wait_send()


def solution(mesh):
    sections, members = mesh.shape["section"], mesh.shape["dp"]

    def on_device(layer_inputs, out_grads, projections, query_grads, lengths):
        seq_len, model_width = layer_inputs.shape[2:]
        rank = projections.shape[2] // 2
        block = query_grads.shape[1]
        flat = query_grads.shape[2]
        group = members // sections
        width = min(128, block * group)
        per = width // block
        half = rank // 2
        slots = sections * group
        step = seq_len // CHUNKS
        return pl.pallas_call(
            functools.partial(kernel, sections, members, width),
            out_shape=jax.ShapeDtypeStruct((1, block * group), jnp.float32),
            in_specs=[pl.BlockSpec(memory_space=pltpu.HBM)] * 5,
            out_specs=pl.BlockSpec(memory_space=pltpu.VMEM),
            scratch_shapes=[
                pltpu.VMEM((CHUNKS, 2 * step, model_width), jnp.bfloat16),
                pltpu.VMEM((model_width, 2 * rank), jnp.bfloat16),
                pltpu.VMEM((width, flat), jnp.bfloat16),
                pltpu.SMEM((1,), jnp.int32),
                pltpu.VMEM((rank, 2 * rank), jnp.float32),
                pltpu.VMEM((members, half, 2 * rank), jnp.bfloat16),
                pltpu.VMEM((members * half, 2 * rank), jnp.float32),
                pltpu.VMEM((members, 1, width), jnp.float32),
                pltpu.VMEM((slots, 1, width), jnp.float32),
                pltpu.SemaphoreType.DMA((CHUNKS, 2)),
                pltpu.SemaphoreType.DMA,
                pltpu.SemaphoreType.DMA((per,)),
                pltpu.SemaphoreType.DMA,
                pltpu.SemaphoreType.DMA((members,)),
                pltpu.SemaphoreType.DMA((members,)),
                pltpu.SemaphoreType.DMA((members,)),
                pltpu.SemaphoreType.DMA((slots,)),
            ],
            compiler_params=pltpu.CompilerParams(
                collective_id=0, has_side_effects=True, vmem_limit_bytes=48 * 1024 * 1024
            ),
            cost_estimate=pl.CostEstimate(
                flops=8 * seq_len * model_width * rank,
                bytes_accessed=4 * seq_len * model_width,
                transcendentals=0,
            ),
        )(layer_inputs, out_grads, projections, query_grads, lengths)

    placed = (
        P("section", "dp", None, None),
        P("section", "dp", None, None),
        P("section", None, None),
        P("section", "dp", None),
        P("dp"),
    )
    return jax.shard_map(
        on_device, mesh=mesh, in_specs=placed, out_specs=P("dp", "section"), check_vma=False
    )
```

time: 87.1 us -> 22.2 us (0.25)
  blocking collectives: 44.1 us -> 0 us
  waiting for transfers between devices: 17 us -> 0 us
  Pallas kernels: 0 us -> 16.5 us
  between operations: 14.2 us -> 0.67 us
  matrix products: 8.15 us -> 0 us
  local copies, waits for them, and re-layouts: 2.72 us -> 4.87 us
    all_gather x1 -> x0, blocking collectives: 32.3 us -> none  [on_device(): lax.all_gather(example_grads, 'dp', axis=1, tiled=True)]
    unnamed x2 -> x0, waiting for transfers between devices: 17 us -> none
    pallas_call x0 -> x1, Pallas kernels: none -> 16.5 us  [on_device(): pl.pallas_call(functools.partial(kernel, sections, members, width), out_s...]
    all_to_all x1 -> x0, blocking collectives: 11.8 us -> none  [on_device(): lax.all_to_all(score_block, 'dp', split_axis=0, concat_axis=1, tiled=True)]
    dot_general x3 -> x0, matrix products: 8.15 us -> none  [the longest x1 4.21 us: project_layer(): jnp.dot(grads.reshape(ex_rows * seq_len, model_width), proj_table[:, low_...]
    unnamed x5 -> x7, local copies, waits for them, and re-layouts: 1.35 us -> 4.87 us
    all_to_all x2 -> x0, local copies, waits for them, and re-layouts: 1.28 us -> none  [on_device(): lax.all_to_all(score_block, 'dp', split_axis=0, concat_axis=1, tiled=True)]
  transfers between devices with their start and end apart: 1 -> 0, of which waited for: 1 -> 0; matrix products, arithmetic and copies ran while one was open for 0% -> 0% of each run, Pallas kernels for 0% -> 0%
where the time goes in v1:
time: 22.2 us; the launch traced here: 22 us
  Pallas kernels  16.5 us (74%)
  local copies, waits for them, and re-layouts  4.87 us (22%)
  between operations  0.67 us (3%)
    pallas_call x1, Pallas kernels, on_device(): pl.pallas_call(functools.partial(kernel, sections, members, width), out_s...  16.5 us
    unnamed x7, local copies, waits for them, and re-layouts  4.87 us

profile of v1, /device:TPU:0, one launch (start us, length us, event | category | flops | bytes accessed | tf_op | source)
XLA Modules:
  0.0 22.0 jit_solution(7081531840844852634)
XLA Ops:
  0.7 0.0 copy-start
  0.7 2.2 %copy-done = bf16[1,1,512,4096]{3,2,1,0:T(8,128)(2,1)S(1)} copy-done((bf16[1,1,512,4096]{3,2,1,0:T(8,128)(2,1)S(1)}, bf16[1,1,512,4096]{3,2,1,0:T(8,128)(2,1)}, u32[]{:S(2)}) %copy-start) | copy-done | bytes 4194328
  2.8 0.0 copy-start.1
  2.8 1.2 %copy-done.1 = bf16[1,4096,128]{2,1,0:T(8,128)(2,1)S(1)} copy-done((bf16[1,4096,128]{2,1,0:T(8,128)(2,1)S(1)}, bf16[1,4096,128]{2,1,0:T(8,128)(2,1)}, u32[]{:S(2)}) %copy-start.1) | copy-done | bytes 1048600
  4.1 0.0 copy-start.2
  4.1 0.9 %copy-done.2 = bf16[1,32,4096]{2,1,0:T(8,128)(2,1)S(1)} copy-done((bf16[1,32,4096]{2,1,0:T(8,128)(2,1)S(1)}, bf16[1,32,4096]{2,1,0:T(8,128)(2,1)}, u32[]{:S(2)}) %copy-start.2) | copy-done | bytes 262168
  5.0 16.5 %shard_map.55 = f32[1,64]{1,0:T(1,128)S(1)} custom-call(bf16[1,1,512,4096]{3,2,1,0:T(8,128)(2,1)S(1)} %copy-done, bf16[1,1,512,4096]{3,2,1,0:T(8,128)(2,1)} %grads_ref.1, bf16[1,4096,128]{2,1,0:T(8,128)(2,1)S(1)} %copy-done.1, bf16[1,32,4096]{2,1,0:T(8,128)(2,1)S(1)} %copy-done.2, s32[1]{0:T(128)S(6)} %copy.7.length_ref), custom_call_target="tpu_custom_call" | custom-call | flops 1073741824 | bytes 8388608 | tf_op jit(solution)/shard_map/pallas_call | solution.py:183
  21.5 0.5 %copy.8 = f32[1,64]{1,0:T(1,128)} copy(f32[1,64]{1,0:T(1,128)S(1)} %shard_map.55) | data formatting | bytes 512
Async XLA Ops:
  0.7 2.2 %copy-start = (bf16[1,1,512,4096]{3,2,1,0:T(8,128)(2,1)S(1)}, bf16[1,1,512,4096]{3,2,1,0:T(8,128)(2,1)}, u32[]{:S(2)}) copy-start(bf16[1,1,512,4096]{3,2,1,0:T(8,128)(2,1)} %inputs_ref.1) | copy-start | bytes 12582916
  2.8 1.2 %copy-start.1 = (bf16[1,4096,128]{2,1,0:T(8,128)(2,1)S(1)}, bf16[1,4096,128]{2,1,0:T(8,128)(2,1)}, u32[]{:S(2)}) copy-start(bf16[1,4096,128]{2,1,0:T(8,128)(2,1)} %proj_ref.1) | copy-start | bytes 3145732
  4.1 0.9 %copy-start.2 = (bf16[1,32,4096]{2,1,0:T(8,128)(2,1)S(1)}, bf16[1,32,4096]{2,1,0:T(8,128)(2,1)}, u32[]{:S(2)}) copy-start(bf16[1,32,4096]{2,1,0:T(8,128)(2,1)} %query_ref.1) | copy-start | bytes 786436

commit v2 on v1

--- a/solution.py
+++ b/solution.py
@@ -14,8 +14,8 @@
 def kernel(
     sections, members, width,
     inputs_ref, grads_ref, proj_ref, query_ref, length_ref, out_ref,
-    rows, proj, query, length, product, packed, spread, scores, parts,
-    row_sem, proj_sem, query_sem, length_sem,
+    rows, proj, query, product, packed, spread, scores, parts,
+    row_sem, proj_sem, query_sem,
     grad_send, grad_recv, score_send, score_recv,
 ):
     sec, dp = lax.axis_index("section"), lax.axis_index("dp")
@@ -29,8 +29,6 @@
     keeps = home == sec
     my_slot = (dp % group) // per * (sections * per) + sec * per + dp % per
 
-    length_copy = pltpu.make_async_copy(length_ref, length, length_sem)
-    length_copy.start()
     proj_copy = pltpu.make_async_copy(proj_ref.at[0], proj, proj_sem)
     proj_copy.start()
     row_copies = []
@@ -67,9 +65,8 @@
             def _():
                 pl.semaphore_signal(barrier, inc=1, device_id=(s, sender), device_id_type=MESH)
 
-    length_copy.wait()
     proj_copy.wait()
-    tokens = length[0]
+    tokens = length_ref[0]
     total = jnp.zeros((2 * rank, 2 * rank), jnp.float32)
     for c in range(CHUNKS):
         for copy in row_copies[c]:
@@ -183,13 +180,12 @@
         return pl.pallas_call(
             functools.partial(kernel, sections, members, width),
             out_shape=jax.ShapeDtypeStruct((1, block * group), jnp.float32),
-            in_specs=[pl.BlockSpec(memory_space=pltpu.HBM)] * 5,
+            in_specs=[pl.BlockSpec(memory_space=pltpu.HBM)] * 4 + [pl.BlockSpec(memory_space=pltpu.SMEM)],
             out_specs=pl.BlockSpec(memory_space=pltpu.VMEM),
             scratch_shapes=[
                 pltpu.VMEM((CHUNKS, 2 * step, model_width), jnp.bfloat16),
                 pltpu.VMEM((model_width, 2 * rank), jnp.bfloat16),
                 pltpu.VMEM((width, flat), jnp.bfloat16),
-                pltpu.SMEM((1,), jnp.int32),
                 pltpu.VMEM((rank, 2 * rank), jnp.float32),
                 pltpu.VMEM((members, half, 2 * rank), jnp.bfloat16),
                 pltpu.VMEM((members * half, 2 * rank), jnp.float32),
@@ -198,14 +194,13 @@
                 pltpu.SemaphoreType.DMA((CHUNKS, 2)),
                 pltpu.SemaphoreType.DMA,
                 pltpu.SemaphoreType.DMA((per,)),
-                pltpu.SemaphoreType.DMA,
                 pltpu.SemaphoreType.DMA((members,)),
                 pltpu.SemaphoreType.DMA((members,)),
                 pltpu.SemaphoreType.DMA((members,)),
                 pltpu.SemaphoreType.DMA((slots,)),
             ],
             compiler_params=pltpu.CompilerParams(
-                collective_id=0, has_side_effects=True, vmem_limit_bytes=48 * 1024 * 1024
+                collective_id=0, has_side_effects=True, vmem_limit_bytes=64 * 1024 * 1024
             ),
             cost_estimate=pl.CostEstimate(
                 flops=8 * seq_len * model_width * rank,

time: 22.2 us -> 21.2 us (0.955)
  local copies, waits for them, and re-layouts: 4.87 us -> 1.19 us
  Pallas kernels: 16.5 us -> 19.2 us
    unnamed x7 -> x1, local copies, waits for them, and re-layouts: 4.87 us -> 1.19 us
    pallas_call x1, Pallas kernels: 16.5 us -> 19.2 us  [on_device(): pl.pallas_call(functools.partial(kernel, sections, members, width), out_s...]
where the time goes in v2:
time: 21.2 us; the launch traced here: 21 us
  Pallas kernels  19.2 us (91%)
  local copies, waits for them, and re-layouts  1.19 us (6%)
  between operations  0.66 us (3%)
    pallas_call x1, Pallas kernels, on_device(): pl.pallas_call(functools.partial(kernel, sections, members, width), out_s...  19.2 us
    unnamed x1, local copies, waits for them, and re-layouts  1.19 us

profile of v2, /device:TPU:0, one launch (start us, length us, event | category | flops | bytes accessed | tf_op | source)
XLA Modules:
  0.0 21.0 jit_solution(3088215772182237038)
XLA Ops:
  0.7 19.2 %shard_map.55 = f32[1,64]{1,0:T(1,128)} custom-call(bf16[1,1,512,4096]{3,2,1,0:T(8,128)(2,1)} %inputs_ref.1, bf16[1,1,512,4096]{3,2,1,0:T(8,128)(2,1)} %grads_ref.1, bf16[1,4096,128]{2,1,0:T(8,128)(2,1)} %proj_ref.1, bf16[1,32,4096]{2,1,0:T(8,128)(2,1)} %query_ref.1, s32[1]{0:T(128)S(6)} %copy.7.length_ref), custom_call_target="tpu_custom_call" | custom-call | flops 1073741824 | bytes 8388608 | tf_op jit(solution)/shard_map/pallas_call | solution.py:180
  19.8 1.2 %copy.8 = f32[1,64]{1,0:T(1,128)} copy(f32[1,64]{1,0:T(1,128)} %shard_map.55) | data formatting | bytes 512

commit v3 on v2

--- a/solution.py
+++ b/solution.py
@@ -14,7 +14,7 @@
 def kernel(
     sections, members, width,
     inputs_ref, grads_ref, proj_ref, query_ref, length_ref, out_ref,
-    rows, proj, query, product, packed, spread, scores, parts,
+    rows, proj, query, total, packed, spread, scores, parts,
     row_sem, proj_sem, query_sem,
     grad_send, grad_recv, score_send, score_recv,
 ):
@@ -31,16 +31,18 @@
 
     proj_copy = pltpu.make_async_copy(proj_ref.at[0], proj, proj_sem)
     proj_copy.start()
-    row_copies = []
-    for c in range(CHUNKS):
-        span = pl.ds(c * step, step)
-        pair = (
-            pltpu.make_async_copy(inputs_ref.at[0, 0, span], rows.at[c, pl.ds(0, step)], row_sem.at[c, 0]),
-            pltpu.make_async_copy(grads_ref.at[0, 0, span], rows.at[c, pl.ds(step, step)], row_sem.at[c, 1]),
-        )
-        for copy in pair:
-            copy.start()
-        row_copies.append(pair)
+
+    def row_copy(c, side, source):
+        return pltpu.make_async_copy(
+            source.at[0, 0, pl.ds(pl.multiple_of(c * step, step), step)],
+            rows.at[c, pl.ds(side * step, step)], row_sem.at[c, side],
+        )
+
+    @pl.loop(0, CHUNKS)
+    def _(c):
+        row_copy(c, 0, inputs_ref).start()
+        row_copy(c, 1, grads_ref).start()
+
     query_copies = []
     for k in range(per):
         copy = pltpu.make_async_copy(query_ref.at[0], query.at[pl.ds(k * block, block)], query_sem.at[k])
@@ -67,20 +69,22 @@
 
     proj_copy.wait()
     tokens = length_ref[0]
-    total = jnp.zeros((2 * rank, 2 * rank), jnp.float32)
-    for c in range(CHUNKS):
-        for copy in row_copies[c]:
-            copy.wait()
+    total[...] = jnp.zeros_like(total)
+
+    @pl.loop(0, CHUNKS)
+    def _(c):
+        row_copy(c, 0, inputs_ref).wait()
+        row_copy(c, 1, grads_ref).wait()
         sides = jnp.dot(rows[c], proj[...], preferred_element_type=jnp.float32).astype(jnp.bfloat16)
         slot = lax.broadcasted_iota(jnp.int32, (step, 2 * rank), 0) + c * step
         masked = jnp.where(slot < tokens, sides[step:].astype(jnp.float32), 0.0).astype(jnp.bfloat16)
-        total += lax.dot_general(
+        total[...] += lax.dot_general(
             masked, sides[:step], (((0,), (0,)), ((), ())), preferred_element_type=jnp.float32
         )
-    product[...] = total[rank:]
+
     half = rank // 2
-    even = product[pl.ds(0, half, stride=2), :]
-    odd = product[pl.ds(1, half, stride=2), :]
+    even = total[pl.ds(rank, half, stride=2), :]
+    odd = total[pl.ds(rank + 1, half, stride=2), :]
     lane = lax.broadcasted_iota(jnp.int32, (half, 2 * rank), 1)
     folded = jnp.where(lane < rank, even, pltpu.roll(odd, rank, 1))
     packed[dp] = (folded / tokens.astype(jnp.float32)).astype(jnp.bfloat16)
@@ -186,7 +190,7 @@
                 pltpu.VMEM((CHUNKS, 2 * step, model_width), jnp.bfloat16),
                 pltpu.VMEM((model_width, 2 * rank), jnp.bfloat16),
                 pltpu.VMEM((width, flat), jnp.bfloat16),
-                pltpu.VMEM((rank, 2 * rank), jnp.float32),
+                pltpu.VMEM((2 * rank, 2 * rank), jnp.float32),
                 pltpu.VMEM((members, half, 2 * rank), jnp.bfloat16),
                 pltpu.VMEM((members * half, 2 * rank), jnp.float32),
                 pltpu.VMEM((members, 1, width), jnp.float32),
@@ -200,7 +204,7 @@
                 pltpu.SemaphoreType.DMA((slots,)),
             ],
             compiler_params=pltpu.CompilerParams(
-                collective_id=0, has_side_effects=True, vmem_limit_bytes=64 * 1024 * 1024
+                collective_id=0, has_side_effects=True, vmem_limit_bytes=(64 * 1024 - 128) * 1024
             ),
             cost_estimate=pl.CostEstimate(
                 flops=8 * seq_len * model_width * rank,

time: 21.2 us -> 19.6 us (0.925)
  Pallas kernels: 19.2 us -> 17.6 us
    pallas_call x1, Pallas kernels: 19.2 us -> 17.6 us  [on_device(): pl.pallas_call(functools.partial(kernel, sections, members, width), out_s...]
where the time goes in v3:
time: 19.6 us; the launch traced here: 19.4 us
  Pallas kernels  17.6 us (90%)
  local copies, waits for them, and re-layouts  1.19 us (6%)
  between operations  0.66 us (3%)
    pallas_call x1, Pallas kernels, on_device(): pl.pallas_call(functools.partial(kernel, sections, members, width), out_s...  17.6 us
    unnamed x1, local copies, waits for them, and re-layouts  1.19 us

profile of v3, /device:TPU:0, one launch (start us, length us, event | category | flops | bytes accessed | tf_op | source)
XLA Modules:
  0.0 19.4 jit_solution(5803372443042390624)
XLA Ops:
  0.7 17.6 %shard_map.55 = f32[1,64]{1,0:T(1,128)} custom-call(bf16[1,1,512,4096]{3,2,1,0:T(8,128)(2,1)} %inputs_ref.1, bf16[1,1,512,4096]{3,2,1,0:T(8,128)(2,1)} %grads_ref.1, bf16[1,4096,128]{2,1,0:T(8,128)(2,1)} %proj_ref.1, bf16[1,32,4096]{2,1,0:T(8,128)(2,1)} %query_ref.1, s32[1]{0:T(128)S(6)} %copy.7.length_ref), custom_call_target="tpu_custom_call" | custom-call | flops 1073741824 | bytes 8388608 | tf_op jit(solution)/shard_map/pallas_call | solution.py:184
  18.2 1.2 %copy.8 = f32[1,64]{1,0:T(1,128)} copy(f32[1,64]{1,0:T(1,128)} %shard_map.55) | data formatting | bytes 512

commit v4 on v3

--- a/solution.py
+++ b/solution.py
@@ -8,19 +8,19 @@
 from jax.sharding import PartitionSpec as P
 
 MESH = pl.DeviceIdType.MESH
-CHUNKS = 4
+CHUNKS = 8
 
 
 def kernel(
     sections, members, width,
     inputs_ref, grads_ref, proj_ref, query_ref, length_ref, out_ref,
-    rows, proj, query, total, packed, spread, scores, parts,
+    rows, proj, query, sides, total, packed, spread, scores, parts,
     row_sem, proj_sem, query_sem,
     grad_send, grad_recv, score_send, score_recv,
 ):
     sec, dp = lax.axis_index("section"), lax.axis_index("dp")
     seq_len = inputs_ref.shape[2]
-    step = seq_len // CHUNKS
+    step = inputs_ref.shape[3] // CHUNKS
     rank = proj_ref.shape[2] // 2
     block = query_ref.shape[1]
     group = members // sections
@@ -29,19 +29,23 @@
     keeps = home == sec
     my_slot = (dp % group) // per * (sections * per) + sec * per + dp % per
 
-    proj_copy = pltpu.make_async_copy(proj_ref.at[0], proj, proj_sem)
-    proj_copy.start()
-
-    def row_copy(c, side, source):
-        return pltpu.make_async_copy(
-            source.at[0, 0, pl.ds(pl.multiple_of(c * step, step), step)],
-            rows.at[c, pl.ds(side * step, step)], row_sem.at[c, side],
+
+    def chunk_copies(c):
+        columns = pl.ds(pl.multiple_of(c * step, step), step)
+        return (
+            pltpu.make_async_copy(proj_ref.at[0, columns], proj.at[c], proj_sem.at[c]),
+            pltpu.make_async_copy(
+                inputs_ref.at[0, 0, :, columns], rows.at[c, pl.ds(0, seq_len)], row_sem.at[c, 0]
+            ),
+            pltpu.make_async_copy(
+                grads_ref.at[0, 0, :, columns], rows.at[c, pl.ds(seq_len, seq_len)], row_sem.at[c, 1]
+            ),
         )
 
     @pl.loop(0, CHUNKS)
     def _(c):
-        row_copy(c, 0, inputs_ref).start()
-        row_copy(c, 1, grads_ref).start()
+        for copy in chunk_copies(c):
+            copy.start()
 
     query_copies = []
     for k in range(per):
@@ -67,24 +71,27 @@
             def _():
                 pl.semaphore_signal(barrier, inc=1, device_id=(s, sender), device_id_type=MESH)
 
-    proj_copy.wait()
-    tokens = length_ref[0]
-    total[...] = jnp.zeros_like(total)
+    sides[...] = jnp.zeros_like(sides)
 
     @pl.loop(0, CHUNKS)
     def _(c):
-        row_copy(c, 0, inputs_ref).wait()
-        row_copy(c, 1, grads_ref).wait()
-        sides = jnp.dot(rows[c], proj[...], preferred_element_type=jnp.float32).astype(jnp.bfloat16)
-        slot = lax.broadcasted_iota(jnp.int32, (step, 2 * rank), 0) + c * step
-        masked = jnp.where(slot < tokens, sides[step:].astype(jnp.float32), 0.0).astype(jnp.bfloat16)
-        total[...] += lax.dot_general(
-            masked, sides[:step], (((0,), (0,)), ((), ())), preferred_element_type=jnp.float32
-        )
-
+        for copy in chunk_copies(c):
+            copy.wait()
+        sides[...] += lax.dot_general(
+            proj[c].T, rows[c], (((1,), (1,)), ((), ())), preferred_element_type=jnp.float32
+        )
+
+    tokens = length_ref[0]
+    slot = lax.broadcasted_iota(jnp.int32, (rank, seq_len), 1)
+    grad_side = sides[pl.ds(rank, rank), pl.ds(seq_len, seq_len)]
+    total[...] = lax.dot_general(
+        jnp.where(slot < tokens, grad_side, 0.0).astype(jnp.bfloat16),
+        sides[:, pl.ds(0, seq_len)].astype(jnp.bfloat16),
+        (((1,), (1,)), ((), ())), preferred_element_type=jnp.float32,
+    )
     half = rank // 2
-    even = total[pl.ds(rank, half, stride=2), :]
-    odd = total[pl.ds(rank + 1, half, stride=2), :]
+    even = total[pl.ds(0, half, stride=2), :]
+    odd = total[pl.ds(1, half, stride=2), :]
     lane = lax.broadcasted_iota(jnp.int32, (half, 2 * rank), 1)
     folded = jnp.where(lane < rank, even, pltpu.roll(odd, rank, 1))
     packed[dp] = (folded / tokens.astype(jnp.float32)).astype(jnp.bfloat16)
@@ -180,23 +187,24 @@
         per = width // block
         half = rank // 2
         slots = sections * group
-        step = seq_len // CHUNKS
+        step = model_width // CHUNKS
         return pl.pallas_call(
             functools.partial(kernel, sections, members, width),
             out_shape=jax.ShapeDtypeStruct((1, block * group), jnp.float32),
             in_specs=[pl.BlockSpec(memory_space=pltpu.HBM)] * 4 + [pl.BlockSpec(memory_space=pltpu.SMEM)],
             out_specs=pl.BlockSpec(memory_space=pltpu.VMEM),
             scratch_shapes=[
-                pltpu.VMEM((CHUNKS, 2 * step, model_width), jnp.bfloat16),
-                pltpu.VMEM((model_width, 2 * rank), jnp.bfloat16),
+                pltpu.VMEM((CHUNKS, 2 * seq_len, step), jnp.bfloat16),
+                pltpu.VMEM((CHUNKS, step, 2 * rank), jnp.bfloat16),
                 pltpu.VMEM((width, flat), jnp.bfloat16),
-                pltpu.VMEM((2 * rank, 2 * rank), jnp.float32),
+                pltpu.VMEM((2 * rank, 2 * seq_len), jnp.float32),
+                pltpu.VMEM((rank, 2 * rank), jnp.float32),
                 pltpu.VMEM((members, half, 2 * rank), jnp.bfloat16),
                 pltpu.VMEM((members * half, 2 * rank), jnp.float32),
                 pltpu.VMEM((members, 1, width), jnp.float32),
                 pltpu.VMEM((slots, 1, width), jnp.float32),
                 pltpu.SemaphoreType.DMA((CHUNKS, 2)),
-                pltpu.SemaphoreType.DMA,
+                pltpu.SemaphoreType.DMA((CHUNKS,)),
                 pltpu.SemaphoreType.DMA((per,)),
                 pltpu.SemaphoreType.DMA((members,)),
                 pltpu.SemaphoreType.DMA((members,)),

time: 19.6 us -> 19.7 us (level)
  no operation moved by 1% of the time
where the time goes in v4:
time: 19.7 us; the launch traced here: 19.5 us
  Pallas kernels  17.7 us (90%)
  local copies, waits for them, and re-layouts  1.19 us (6%)
  between operations  0.66 us (3%)
    pallas_call x1, Pallas kernels, on_device(): pl.pallas_call(functools.partial(kernel, sections, members, width), out_s...  17.7 us
    unnamed x1, local copies, waits for them, and re-layouts  1.19 us

profile of v4, /device:TPU:0, one launch (start us, length us, event | category | flops | bytes accessed | tf_op | source)
XLA Modules:
  0.0 19.5 jit_solution(16567787576203276752)
XLA Ops:
  0.7 17.7 %shard_map.55 = f32[1,64]{1,0:T(1,128)} custom-call(bf16[1,1,512,4096]{3,2,1,0:T(8,128)(2,1)} %inputs_ref.1, bf16[1,1,512,4096]{3,2,1,0:T(8,128)(2,1)} %grads_ref.1, bf16[1,4096,128]{2,1,0:T(8,128)(2,1)} %proj_ref.1, bf16[1,32,4096]{2,1,0:T(8,128)(2,1)} %query_ref.1, s32[1]{0:T(128)S(6)} %copy.7.length_ref), custom_call_target="tpu_custom_call" | custom-call | flops 1073741824 | bytes 8388608 | tf_op jit(solution)/shard_map/pallas_call | solution.py:191
  18.3 1.2 %copy.8 = f32[1,64]{1,0:T(1,128)} copy(f32[1,64]{1,0:T(1,128)} %shard_map.55) | data formatting | bytes 512

commit v5 on v4

--- a/solution.py
+++ b/solution.py
@@ -188,6 +188,10 @@
         half = rank // 2
         slots = sections * group
         step = model_width // CHUNKS
+        held = [
+            pltpu.with_memory_space_constraint(array, pltpu.HBM)
+            for array in (layer_inputs, out_grads, projections, query_grads)
+        ]
         return pl.pallas_call(
             functools.partial(kernel, sections, members, width),
             out_shape=jax.ShapeDtypeStruct((1, block * group), jnp.float32),
@@ -212,14 +216,14 @@
                 pltpu.SemaphoreType.DMA((slots,)),
             ],
             compiler_params=pltpu.CompilerParams(
-                collective_id=0, has_side_effects=True, vmem_limit_bytes=(64 * 1024 - 128) * 1024
+                collective_id=0, has_side_effects=True, vmem_limit_bytes=48 * 1024 * 1024
             ),
             cost_estimate=pl.CostEstimate(
                 flops=8 * seq_len * model_width * rank,
                 bytes_accessed=4 * seq_len * model_width,
                 transcendentals=0,
             ),
-        )(layer_inputs, out_grads, projections, query_grads, lengths)
+        )(*held, lengths)
 
     placed = (
         P("section", "dp", None, None),

time: 19.7 us -> 18.4 us (0.934)
  local copies, waits for them, and re-layouts: 1.19 us -> 0.51 us
  Pallas kernels: 17.7 us -> 17.1 us
    unnamed x1, local copies, waits for them, and re-layouts: 1.19 us -> 0.51 us
    pallas_call x1, Pallas kernels: 17.7 us -> 17.1 us  [on_device(): pl.pallas_call(functools.partial(kernel, sections, members, width), out_s...]
where the time goes in v5:
time: 18.4 us; the launch traced here: 18.2 us
  Pallas kernels  17.1 us (93%)
  between operations  0.66 us (4%)
  local copies, waits for them, and re-layouts  0.51 us (3%)
    pallas_call x1, Pallas kernels, on_device(): pl.pallas_call(functools.partial(kernel, sections, members, width), out_s...  17.1 us
    unnamed x1, local copies, waits for them, and re-layouts  0.51 us

profile of v5, /device:TPU:0, one launch (start us, length us, event | category | flops | bytes accessed | tf_op | source)
XLA Modules:
  0.0 18.2 jit_solution(3394197809526972429)
XLA Ops:
  0.7 17.1 %shard_map.55 = f32[1,64]{1,0:T(1,128)S(1)} custom-call(bf16[1,1,512,4096]{3,2,1,0:T(8,128)(2,1)} %inputs_ref.1, bf16[1,1,512,4096]{3,2,1,0:T(8,128)(2,1)} %grads_ref.1, bf16[1,4096,128]{2,1,0:T(8,128)(2,1)} %proj_ref.1, bf16[1,32,4096]{2,1,0:T(8,128)(2,1)} %query_ref.1, s32[1]{0:T(128)S(6)} %copy.7.length_ref), custom_call_target="tpu_custom_call" | custom-call | flops 1073741824 | bytes 8388608 | tf_op jit(solution)/shard_map/pallas_call | solution.py:195
  17.7 0.5 %copy.8 = f32[1,64]{1,0:T(1,128)} copy(f32[1,64]{1,0:T(1,128)S(1)} %shard_map.55) | data formatting | bytes 512

commit v6 on v5

--- a/solution.py
+++ b/solution.py
@@ -8,7 +8,7 @@
 from jax.sharding import PartitionSpec as P
 
 MESH = pl.DeviceIdType.MESH
-CHUNKS = 8
+CHUNKS = 4
 
 
 def kernel(

time: 18.4 us -> 18.2 us (0.989)
  Pallas kernels: 17.1 us -> 16.8 us
    pallas_call x1, Pallas kernels: 17.1 us -> 16.8 us  [on_device(): pl.pallas_call(functools.partial(kernel, sections, members, width), out_s...]
where the time goes in v6:
time: 18.2 us; the launch traced here: 18 us
  Pallas kernels  16.8 us (92%)
  between operations  0.66 us (4%)
  local copies, waits for them, and re-layouts  0.51 us (3%)
    pallas_call x1, Pallas kernels, on_device(): pl.pallas_call(functools.partial(kernel, sections, members, width), out_s...  16.8 us
    unnamed x1, local copies, waits for them, and re-layouts  0.51 us

profile of v6, /device:TPU:0, one launch (start us, length us, event | category | flops | bytes accessed | tf_op | source)
XLA Modules:
  0.0 18.0 jit_solution(13658957559713490464)
XLA Ops:
  0.7 16.8 %shard_map.55 = f32[1,64]{1,0:T(1,128)S(1)} custom-call(bf16[1,1,512,4096]{3,2,1,0:T(8,128)(2,1)} %inputs_ref.1, bf16[1,1,512,4096]{3,2,1,0:T(8,128)(2,1)} %grads_ref.1, bf16[1,4096,128]{2,1,0:T(8,128)(2,1)} %proj_ref.1, bf16[1,32,4096]{2,1,0:T(8,128)(2,1)} %query_ref.1, s32[1]{0:T(128)S(6)} %copy.7.length_ref), custom_call_target="tpu_custom_call" | custom-call | flops 1073741824 | bytes 8388608 | tf_op jit(solution)/shard_map/pallas_call | solution.py:195
  17.5 0.5 %copy.8 = f32[1,64]{1,0:T(1,128)} copy(f32[1,64]{1,0:T(1,128)S(1)} %shard_map.55) | data formatting | bytes 512
